TPU v7x, 512 devices: a whole 4x4x16 slice. The times are simulated.
512 devices in a mesh: prompt: 16 (over z), resp: 16 (over y_lo, x, core), tp: 2 (over y_hi).
Axes of the slice: x: 4, y: 4 (y_hi: 2, y_lo: 2; y = y_hi * 2 + y_lo), z: 16, core: 2. Of those that a mesh axis runs over, the one named last changes fastest.
Arguments:
- prefix_query: bfloat16 [32768, 5120], P(('prompt', 'resp'), 'tp'), parts along dimension 0, may hold values from -8 to 8
- prefix_cache: bfloat16 [2, 32768, 1024], P(None, ('prompt', 'resp', 'tp')), parts along dimension 1, may hold values from -8 to 8
- response_query: bfloat16 [256, 256, 5120], P(('prompt', 'resp'), None, 'tp'), parts along dimension 0, may hold values from -8 to 8
- response_key_value_cache: bfloat16 [2, 256, 256, 1024], P(None, ('prompt', 'resp'), None, 'tp'), parts along dimension 1, may hold values from -6 to 6
- response_tiles: int32 [256], P(('prompt', 'resp')), parts along dimension 0, may hold values from 1 to 2, as said below
- prefix_mask: int32 [256, 2, 16], P(('prompt', 'resp')), parts along dimension 0, may hold values 0 or 1
- self_mask: int32 [256, 2, 2], P(('prompt', 'resp')), parts along dimension 0, may hold values 0 or 1
Outputs:
- prefix_attended: bfloat16 [32768, 5120], P(('prompt', 'resp'), 'tp'), parts along dimension 0
- response_attended: bfloat16 [256, 256, 5120], P(('prompt', 'resp'), None, 'tp'), parts along dimension 0
There are 16 independent parts, one for each index of `prompt`. A program takes and returns all parts, laid end to end along the dimension named above; each array names one. Nothing has to cross between parts.
Inputs may be any that keep to these rules, and one draw needn't show every extreme that they name: `response_tiles`: at least one response of every prompt has exactly 2 live tiles, and at least one other has exactly 1. `self_mask`: only entries of tiles before the query's tile are read.
All inputs are finite; a program needn't handle non-finite values. No bound on the sum of `prefix_mask` or of `self_mask` on one device may be relied on, other than what follows from the above.
Results may differ from a plain program's by a relative error of at most 0.009.
Values may be sent and summed in bfloat16 or wider, within the bound.
No kernel may reach another device: no remote copies, remote signals or barrier semaphores. Data moves between devices by JAX's collectives and lax.ppermute only.
A program may use at most 128 MiB of HBM per device.

v0:
```python
import jax
import jax.numpy as jnp
from jax import lax
from jax.sharding import PartitionSpec as P

QUERY_HEADS = 40
KEY_VALUE_HEADS = 8
HEAD_WIDTH = 128
TILE_TOKENS = 128


NEG_FILL = -1e30


def block_width(row_number):
    return max(
        (divisor for divisor in range(1, min(row_number, 128) + 1) if row_number % divisor == 0)
    )


def merge_block(running, query_rows, key_block, value_block, visible, score_scale):
    maxima, totals, summed = running
    scores = (
        jnp.einsum("rghd,kgd->ghrk", query_rows, key_block, preferred_element_type=jnp.float32)
        * score_scale
    )
    block_max = jnp.max(jnp.where(visible, scores, NEG_FILL), axis=-1)
    new_max = jnp.maximum(maxima, block_max)
    weights = jnp.where(visible, jnp.exp(scores - new_max[..., None]), 0.0)
    factor = jnp.exp(maxima - new_max)
    totals = totals * factor + jnp.sum(weights, axis=-1)
    rounded = weights.astype(jnp.bfloat16)
    update = jnp.einsum("ghrk,kgd->rghd", rounded, value_block, preferred_element_type=jnp.float32)
    summed = summed * jnp.transpose(factor, (2, 0, 1))[..., None] + update
    return (new_max, totals, summed)


def attend_keys(running, query_rows, key_matrix, value_matrix, visible_fn, score_scale):
    row_number = key_matrix.shape[0]
    block_rows = block_width(row_number)
    blocks = row_number // block_rows
    key_blocks = key_matrix.reshape(blocks, block_rows, key_matrix.shape[1], key_matrix.shape[2])
    value_blocks = value_matrix.reshape(
        blocks, block_rows, value_matrix.shape[1], value_matrix.shape[2]
    )

    def advance(state_now, inputs):
        block_index, key_block, value_block = inputs
        visible = visible_fn(block_index * block_rows, block_rows)
        return (
            merge_block(state_now, query_rows, key_block, value_block, visible, score_scale),
            None,
        )

    result, unused = lax.scan(
        advance, running, (jnp.arange(blocks, dtype=jnp.int32), key_blocks, value_blocks)
    )
    return result


def take_rows(running):
    return (running[0], running[1], running[2])


def put_rows(section):
    return (section[0], section[1], section[2])


def finish(running, live_rows):
    maxima, totals, summed = running
    divisor = jnp.where(live_rows[None, None, :], totals, 1.0)
    scaled = summed / jnp.transpose(divisor, (2, 0, 1))[..., None]
    return jnp.where(live_rows[:, None, None, None], scaled, 0.0).astype(jnp.bfloat16)


def over_rows(running, response_len, row_step):
    return row_step(running, 0, response_len)


def shards(
    prefix_query,
    prefix_cache,
    response_query,
    response_key_value_cache,
    response_tiles,
    prefix_mask,
    self_mask,
):
    group_members = QUERY_HEADS // KEY_VALUE_HEADS
    score_scale = HEAD_WIDTH ** (-0.5)
    heads_here = prefix_query.shape[1] // HEAD_WIDTH
    groups_here = heads_here // group_members
    prefill_rows = prefix_query.shape[0]
    response_len = response_query.shape[1]
    tile_total = response_len // TILE_TOKENS
    prompt_tiles = prefix_mask.shape[2]
    group_rank = lax.axis_index("resp")
    pair_rank = lax.axis_index("tp")
    prefill_queries = prefix_query.reshape(prefill_rows, groups_here, group_members, HEAD_WIDTH)
    prefill_pos = group_rank * prefill_rows + jnp.arange(prefill_rows, dtype=jnp.int32)
    own_queries = response_query[0].reshape(response_len, groups_here, group_members, HEAD_WIDTH)
    own_keys = response_key_value_cache[0, 0].reshape(response_len, groups_here, HEAD_WIDTH)
    own_values = response_key_value_cache[1, 0].reshape(response_len, groups_here, HEAD_WIDTH)
    live_tiles = response_tiles[0]
    row_tile = jnp.arange(response_len, dtype=jnp.int32) // TILE_TOKENS
    live_rows = row_tile < live_tiles
    row_onehot = (row_tile[:, None] == jnp.arange(tile_total, dtype=jnp.int32)[None, :]).astype(
        jnp.float32
    )
    prompt_rows_mask = jnp.dot(row_onehot, prefix_mask[0].astype(jnp.float32))
    own_rows_mask = jnp.dot(row_onehot, self_mask[0].astype(jnp.float32))

    def empty_state(row_number):
        return (
            jnp.full((groups_here, group_members, row_number), NEG_FILL, jnp.float32),
            jnp.zeros((groups_here, group_members, row_number), jnp.float32),
            jnp.zeros((row_number, groups_here, group_members, HEAD_WIDTH), jnp.float32),
        )

    def own_step(state_now, row_start, row_number):
        section = take_rows(state_now)
        query_pos = row_start + jnp.arange(row_number, dtype=jnp.int32)
        query_tile = query_pos // TILE_TOKENS

        def own_visible(offset, block_rows):
            key_pos = offset + jnp.arange(block_rows, dtype=jnp.int32)
            key_tile = key_pos // TILE_TOKENS
            key_onehot = (
                key_tile[:, None] == jnp.arange(tile_total, dtype=jnp.int32)[None, :]
            ).astype(jnp.float32)
            allowed = jnp.dot(own_rows_mask, key_onehot.T) > 0.5
            same_tile = key_tile[None, :] == query_tile[:, None]
            causal = key_pos[None, :] <= query_pos[:, None]
            return causal & (same_tile | allowed) & live_rows[:, None]

        section = attend_keys(section, own_queries, own_keys, own_values, own_visible, score_scale)
        return put_rows(section)

    response_state = over_rows(empty_state(response_len), response_len, own_step)
    chosen = lax.dynamic_slice_in_dim(
        lax.all_gather(prefix_cache, ("resp", "tp"), axis=1, tiled=True),
        pair_rank * groups_here * HEAD_WIDTH,
        groups_here * HEAD_WIDTH,
        2,
    )
    first_row = jnp.int32(0)
    prefill_state = empty_state(prefill_rows)
    response_now = response_state
    key_matrix = chosen[0].reshape(chosen.shape[1], groups_here, HEAD_WIDTH)
    value_matrix = chosen[1].reshape(chosen.shape[1], groups_here, HEAD_WIDTH)

    def prefill_visible(offset, block_rows):
        key_pos = first_row + offset + jnp.arange(block_rows, dtype=jnp.int32)
        return key_pos[None, :] <= prefill_pos[:, None]

    prefill_state = attend_keys(
        prefill_state, prefill_queries, key_matrix, value_matrix, prefill_visible, score_scale
    )

    def response_step(state_now, row_start, row_number):
        section = take_rows(state_now)

        def response_visible(offset, block_rows):
            key_tile = (first_row + offset + jnp.arange(block_rows, dtype=jnp.int32)) // TILE_TOKENS
            key_onehot = (
                key_tile[:, None] == jnp.arange(prompt_tiles, dtype=jnp.int32)[None, :]
            ).astype(jnp.float32)
            return (jnp.dot(prompt_rows_mask, key_onehot.T) > 0.5) & live_rows[:, None]

        section = attend_keys(
            section, own_queries, key_matrix, value_matrix, response_visible, score_scale
        )
        return put_rows(section)

    response_now = over_rows(response_now, response_len, response_step)
    prefill_state, response_state = (prefill_state, response_now)
    prefill_done = finish(prefill_state, jnp.ones((prefill_rows,), dtype=jnp.bool_)).reshape(
        prefill_rows, heads_here * HEAD_WIDTH
    )
    response_done = finish(response_state, live_rows).reshape(
        1, response_len, heads_here * HEAD_WIDTH
    )
    return (prefill_done, response_done)


def solution(mesh):
    placed = (
        P(("prompt", "resp"), "tp"),
        P(None, ("prompt", "resp", "tp"), None),
        P(("prompt", "resp"), None, "tp"),
        P(None, ("prompt", "resp"), None, "tp"),
        P(("prompt", "resp")),
        P(("prompt", "resp"), None, None),
        P(("prompt", "resp"), None, None),
    )
    return jax.shard_map(
        shards,
        mesh=mesh,
        in_specs=placed,
        out_specs=(P(("prompt", "resp"), "tp"), P(("prompt", "resp"), None, "tp")),
        check_vma=False,
    )
```

profile of v0, /device:TPU:1, one launch (start us, length us, event | category | flops | bytes accessed | tf_op | source)
XLA Modules:
  0.0 325.9 jit_solution(10307649284262729741)
XLA Ops:
  16.8 26.0 %while.51 = (s32[]{:T(128)}, f32[4,5,256]{2,1,0:T(8,128)S(1)}, f32[4,5,256]{2,1,0:T(8,128)S(1)}, f32[256,4,5,128]{0,3,2,1:T(8,128)}, s32[2]{0:T(128)}, /*index=5...) while((s32[]{:T(128)}, f32[4,5,256]{2,1,0:T(8,128)S(1)}, ...), condition=%wide.region_7.8_spmd.clone, body=%wide.region_4.7_spmd.clone.sunk | while | flops 345084416 | bytes 15931053 | solution.py:55
  20.2 1.7 constant_dynamic-slice_fusion.5
  21.9 1.9 fusion.132
  25.5 3.2 bitcast_add_fusion.5
  32.7 1.7 constant_dynamic-slice_fusion.5
  34.4 1.9 fusion.132
  38.0 4.2 %bitcast_add_fusion.5 = f32[256,4,5,128]{0,3,2,1:T(8,128)} fusion(f32[256,4,5,128]{0,3,2,1:T(8,128)} %get-tuple-element.808, f32[4,128,256,5]{2,1,3,0:T(8,128)S(1)} %get-tuple-element.753, f32[256,4,5]{0,2,1:T(8,128)} %get-tuple-element.754, f32[4,5,256]{2,1,0:T(8,128)S(1)} %get-tuple-element.819, pred[]{:T(512)S(6)} %compare.46, ...), kind=kOutput, calls=%fused_computation.70.clone.1 | convolution fusion | flops 172359680 | bytes 8069121 | tf_op jit(solution)/shard_map/while/body/eval_jaxpr/ghrk,kgd->rghd/dot_general | solution.py:33
  42.8 72.6 %all-gather.2.cloned.1.call-done = bf16[2,2048,1024]{2,1,0:T(8,128)(2,1)} async-done(((bf16[2,64,1024]{2,1,0:T(8,128)(2,1)}), bf16[2,2048,1024]{2,1,0:T(8,128)(2,1)}) %all-gather.2.cloned.1.call-update) | async-done | bytes 8388624 | tf_op jit(solution)/shard_map/all_gather | solution.py:141
  115.4 3.9 %constant_dynamic-slice_fusion.3 = (bf16[1,2048,512]{2,1,0:T(8,128)(2,1)S(1)}, bf16[1,2048,512]{2,1,0:T(8,128)(2,1)}) fusion(bf16[2,2048,1024]{2,1,0:T(8,128)(2,1)} %all-gather.2.cloned.1.call-done, s32[]{:T(128)S(6)} %add.165, s32[]{:T(128)S(6)} %select_n.100), kind=kLoop, calls=%fused_computation.131 | loop fusion | bytes 8388616 | tf_op jit(solution)/shard_map/slice | solution.py:150
  119.3 4.0 %reshape.147 = bf16[16,128,4,128]{3,2,1,0:T(4,128)(2,1)} reshape(bf16[1,2048,512]{2,1,0:T(8,128)(2,1)} %get-tuple-element.540) | data formatting | bytes 4194304 | tf_op jit(solution)/shard_map/reshape;reshape;squeeze | solution.py:42
  123.2 3.5 %copy.20 = bf16[16,128,4,128]{3,1,2,0:T(8,128)(2,1)} copy(bf16[16,128,4,128]{3,2,1,0:T(4,128)(2,1)} %reshape.147) | data formatting | bytes 4194304
  126.7 2.1 reshape.148
  128.8 4.3 %copy.22 = bf16[16,128,4,128]{1,3,2,0:T(8,128)(2,1)} copy(bf16[16,128,4,128]{3,2,1,0:T(4,128)(2,1)} %reshape.148) | data formatting | bytes 4194304
  133.1 108.3 %while.49 = (s32[]{:T(128)}, f32[4,5,256]{2,1,0:T(8,128)S(1)}, f32[4,5,256]{2,1,0:T(8,128)S(1)}, f32[256,4,5,128]{0,3,2,1:T(8,128)S(1)}, s32[16]{0:T(128)S(1)}, ...) while((s32[]{:T(128)}, f32[4,5,256]{2,1,0:T(8,128)S(1)}, ...), condition=%wide.region_11.12_spmd.clone, body=%wide.region_8.11_spmd.clone.sunk | while | flops 345199872 | bytes 15149717 | solution.py:55
  135.3 1.9 fusion.117
  137.3 2.0 bitcast_add_fusion.4
  142.1 1.9 fusion.117
  144.0 2.0 bitcast_add_fusion.4
  148.8 1.9 fusion.117
  150.8 2.0 bitcast_add_fusion.4
  155.6 1.9 fusion.117
  157.6 2.0 bitcast_add_fusion.4
  162.4 1.9 fusion.117
  164.3 2.0 bitcast_add_fusion.4
  169.1 1.9 fusion.117
  171.1 2.0 bitcast_add_fusion.4
  175.9 1.9 fusion.117
  177.9 2.0 bitcast_add_fusion.4
  182.7 1.9 fusion.117
  184.7 2.0 bitcast_add_fusion.4
  189.4 1.9 fusion.117
  191.4 2.0 bitcast_add_fusion.4
  196.2 1.9 fusion.117
  198.2 2.0 bitcast_add_fusion.4
  203.0 1.9 fusion.117
  205.0 2.0 bitcast_add_fusion.4
  209.8 1.9 fusion.117
  211.7 2.0 bitcast_add_fusion.4
  216.5 1.9 fusion.117
  218.5 2.0 bitcast_add_fusion.4
  223.3 1.9 fusion.117
  225.3 2.0 bitcast_add_fusion.4
  230.1 1.9 fusion.117
  232.0 2.0 bitcast_add_fusion.4
  236.8 1.9 fusion.117
  238.8 2.0 bitcast_add_fusion.4
  242.9 2.5 copy.31
  245.4 72.4 %while.50 = (s32[]{:T(128)}, f32[4,5,128]{2,1,0:T(8,128)S(1)}, f32[4,5,128]{2,1,0:T(8,128)S(1)}, f32[128,4,5,128]{0,3,2,1:T(8,128)S(1)}, s32[16]{0:T(128)S(1)}, ...) while((s32[]{:T(128)}, f32[4,5,128]{2,1,0:T(8,128)S(1)}, ...), condition=%wide.region_3.4_spmd.clone, body=%wide.region_0.3_spmd.clone.sunk | while | flops 171736320 | bytes 7703713 | solution.py:55
  (336 shorter events, 115.3 us)
Async XLA Ops:
  7.2 108.2 %all-gather.2.cloned.1.call-start = ((), (), s32[]{:S(2)}) async-start(), calls=%async_computation | async-start | bytes 8650752 | tf_op jit(solution)/shard_map/all_gather | solution.py:141
  8.0 3.1 copy-start.4
  9.6 3.7 %copy-start.2 = (bf16[128,2560]{1,0:T(8,128)(2,1)S(1)}, bf16[128,2560]{1,0:T(8,128)(2,1)}, u32[]{:S(2)}) copy-start(bf16[128,2560]{1,0:T(8,128)(2,1)} %param.13) | copy-start | bytes 1966084
  11.1 3.5 %copy-start.6 = (s32[1,2,2]{2,1,0:T(2,128)S(1)}, s32[1,2,2]{2,1,0:T(2,128)}, u32[]{:S(2)}) copy-start(s32[1,2,2]{2,1,0:T(2,128)} %param.19) | copy-start | bytes 52
  11.1 4.3 %copy-start.7 = (s32[1,2,16]{2,1,0:T(2,128)S(1)}, s32[1,2,16]{2,1,0:T(2,128)}, u32[]{:S(2)}) copy-start(s32[1,2,16]{2,1,0:T(2,128)} %param.18) | copy-start | bytes 388
  128.8 4.3 %copy-start = (f32[256,4,5,128]{0,3,2,1:T(8,128)S(1)}, f32[256,4,5,128]{0,3,2,1:T(8,128)}, u32[]{:S(2)}) copy-start(f32[256,4,5,128]{0,3,2,1:T(8,128)} %get-tuple-element.834) | copy-start | bytes 7864324
  128.8 4.3 %copy-start.8 = (bf16[256,16]{0,1:T(8,128)(2,1)S(1)}, bf16[256,16]{0,1:T(8,128)(2,1)}, u32[]{:S(2)}) copy-start(bf16[256,16]{0,1:T(8,128)(2,1)} %fusion.72) | copy-start | bytes 24580
  133.1 108.4 %copy-start.5 = (pred[256]{0:T(512)(128)(4,1)S(1)}, pred[256]{0:T(512)(128)(4,1)}, u32[]{:S(2)}) copy-start(pred[256]{0:T(512)(128)(4,1)} %broadcast_compare_fusion.2) | copy-start | bytes 772
  241.5 3.9 %copy-start.3 = (f32[4,5,128]{2,1,0:T(8,128)S(1)}, f32[4,5,128]{2,1,0:T(8,128)}, u32[]{:S(2)}) copy-start(f32[4,5,128]{2,1,0:T(8,128)} %custom-call.1) | copy-start | bytes 30724
  242.9 2.5 copy-start.1
Sparse Core Ops, SparseCore 0:
  10.1 105.2 all-gather.1
where the time goes:
time: 328 us; the launch traced here: 326 us
  matrix products  127 us (39%)
  waiting for transfers between devices  73.3 us (22%)
  local copies, waits for them, and re-layouts  54 us (16%)
  other arithmetic  31.9 us (10%)
  loops' own time  24.7 us (8%)
  between operations  14.9 us (5%)
    all_gather x1, waiting for transfers between devices, shards(): lax.all_gather(prefix_cache, ('resp', 'tp'), axis=1, tiled=True)  72.6 us
    dot_general x34, matrix products, merge_block(): jnp.einsum('ghrk,kgd->rghd', rounded, value_block, preferred_element_type...  64.8 us
    dot_general x34, matrix products, merge_block(): jnp.einsum('rghd,kgd->ghrk', query_rows, key_block, preferred_element_typ...  55.6 us
    dynamic_slice x38, local copies, waits for them, and re-layouts, attend_keys(): lax.scan(advance, running, (jnp.arange(blocks, dtype=jnp.int32), key_bloc...  26.7 us
    another operation x3, loops' own time, attend_keys(): lax.scan(advance, running, (jnp.arange(blocks, dtype=jnp.int32), key_bloc...  24.7 us
    unnamed x26, local copies, waits for them, and re-layouts  15.2 us
    reduce_sum x34, other arithmetic, merge_block(): totals = totals * factor + jnp.sum(weights, axis=-1)  14 us
    lt x19, other arithmetic, shards(): live_rows = row_tile < live_tiles  12.4 us
  transfers between devices with their start and end apart: 1, of which 1 were waited for; matrix products, arithmetic and copies ran while one was open for 10% of the time, Pallas kernels for 0%

commit v1 on v0

v1 whole, which is shorter than its diff:
```python
import functools
import math

import jax
import jax.numpy as jnp
from jax import lax
from jax.experimental import pallas as pl
from jax.experimental.pallas import tpu as pltpu
from jax.sharding import PartitionSpec as P

QUERY_HEADS = 40
KEY_VALUE_HEADS = 8
HEAD_WIDTH = 128
TILE = 128
MEMBERS = QUERY_HEADS // KEY_VALUE_HEADS
GROUPS = KEY_VALUE_HEADS // 2
HALF = GROUPS * HEAD_WIDTH
PROMPT_TILES = 16
OWN_TILES = 2
KEY_TILES = PROMPT_TILES + OWN_TILES
PART = 64
ROWS = MEMBERS * TILE
SCALE = HEAD_WIDTH**-0.5
SCALE2 = SCALE * math.log2(math.e)
NEG_FILL = -1e30
AX = ("resp", "tp")
SIZES = (8, 12, 14, 16, 18)
CHUNK = 4


def rank_of(x, y, core):
    return (((y % 2) * 4 + x) * 2 + core) * 2 + y // 2


def pairs(flip):
    return [
        (rank_of(x, y, core), rank_of(*flip(x, y, core)))
        for x in range(4)
        for y in range(4)
        for core in range(2)
    ]


def first_pairs(m):
    return pairs(lambda x, y, core: (x, y ^ m, core) if core == 0 else (x ^ m, y, core))


def second_pairs(m):
    return pairs(lambda x, y, core: (x ^ m, y, core) if core == 0 else (x, y ^ m, core))


CORE_PAIRS = pairs(lambda x, y, core: (x, y, 1 - core))


def gather_prompt(cache, half, core):
    got = [cache] + [lax.ppermute(cache, AX, first_pairs(m)) for m in (1, 2, 3)]
    stacked = jnp.stack(got)
    mine = lax.dynamic_slice_in_dim(stacked, half * HALF, HALF, 3)
    far = jnp.where(core == 0, half, 1 - half)
    other = lax.dynamic_slice_in_dim(stacked, far * HALF, HALF, 3)
    same_core = [mine] + [
        lax.ppermute(mine if m == 1 else other, AX, second_pairs(m)) for m in (1, 2, 3)
    ]
    other_core = [lax.ppermute(a, AX, CORE_PAIRS) for a in same_core]
    return same_core, other_core


def attend_kernel(
    place,
    prefix_mask,
    self_mask,
    prefix_q,
    response_q,
    own_kv,
    *rest,
):
    pieces = rest[:8]
    prefix_out, response_out = rest[8:10]
    keys, values, values_t, queries, sums, acc, row_max, row_sum, lists, counts = rest[10:]
    x, y, core, rank, live = (place[i] for i in range(5))

    @pl.when(pl.program_id(0) == 0)
    def _():
        for t in range(3):
            for i in range(KEY_TILES):
                lists[t, i] = jnp.int32(0)
            lists[t, 0] = rank if t == 0 else jnp.int32(PROMPT_TILES + t - 1)

            def put(seen, tile, count, t=t):
                lists[t, count] = tile
                return count + jnp.where(seen, 1, 0)

            def step(j, count, t=t, put=put):
                seen = j < rank if t == 0 else prefix_mask[t - 1, j] == 1
                return put(seen, j, count)

            count = lax.fori_loop(0, PROMPT_TILES, step, jnp.int32(1))
            if t == 2:
                count = put(self_mask[1, 0] == 1, PROMPT_TILES, count)
            counts[t] = count

    for index, piece in enumerate(pieces):
        from_core = core if index < 4 else 1 - core
        m = index % 4
        for j in range(4):
            source_x = jnp.where(from_core == 0, x ^ m, x ^ j)
            source_y = jnp.where(from_core == 0, y ^ j, y ^ m)
            tile = ((source_y & 1) * 4 + source_x) * 2 + from_core
            start = pl.multiple_of((source_y >> 1) * PART, PART)
            keys[tile, pl.ds(start, PART), :] = piece[j, 0]
            values[tile, pl.ds(start, PART), :] = piece[j, 1]
    for i in range(OWN_TILES):
        keys[PROMPT_TILES + i] = own_kv[0, i * TILE : (i + 1) * TILE, :]
        values[PROMPT_TILES + i] = own_kv[1, i * TILE : (i + 1) * TILE, :]
    for i in range(KEY_TILES):
        values_t[i] = values[i].T
    for t in range(3):
        for h in range(MEMBERS):
            columns = slice(h * HEAD_WIDTH, (h + 1) * HEAD_WIDTH)
            block = prefix_q[:, columns] if t == 0 else response_q[(t - 1) * TILE : t * TILE, columns]
            queries[t, h * TILE : (h + 1) * TILE, :] = block

    def store(t, h, block):
        columns = slice(h * HEAD_WIDTH, (h + 1) * HEAD_WIDTH)

        @pl.when(t == 0)
        def _():
            prefix_out[:, columns] = block

        @pl.when(t > 0)
        def _():
            start = pl.multiple_of((t - 1) * TILE, TILE)
            response_out[pl.ds(start, TILE), columns] = block

    def scores(a, b):
        return lax.dot_general(a, b, (((1,), (1,)), ((), ())), preferred_element_type=jnp.float32)

    def attend(t, size, sure):
        count = counts[t]
        q = queries[t]
        tiles = [lists[t, i] for i in range(size)]
        causal = lax.broadcasted_iota(jnp.int32, (TILE, TILE), 0) <= lax.broadcasted_iota(
            jnp.int32, (TILE, TILE), 1
        )
        causal = jnp.concatenate([causal] * MEMBERS, axis=1)
        weights, total = [], None
        for start in range(0, size, CHUNK):
            chunk = range(start, min(start + CHUNK, size))
            k = jnp.concatenate([keys[tiles[i]] for i in chunk], axis=0)
            part = jnp.exp2(scores(k, q) * SCALE2)
            for i in chunk:
                block = part[(i - start) * TILE : (i - start + 1) * TILE]
                if i == 0:
                    block = jnp.where(causal, block, 0.0)
                elif i >= sure:
                    block = jnp.where(i < count, block, 0.0)
                folded = jnp.sum(block.reshape(TILE // 8, 8, ROWS), axis=0)
                total = folded if total is None else total + folded
                weights.append(block.astype(jnp.bfloat16))
        v = jnp.concatenate([values_t[tile] for tile in tiles], axis=1)
        summed = jnp.dot(v, jnp.concatenate(weights, axis=0), preferred_element_type=jnp.float32)
        total = jnp.sum(total, axis=0, keepdims=True)
        sums[0:1, :] = jnp.minimum(sums[0:1, :], total)
        sums[1:2, :] = jnp.maximum(sums[1:2, :], total)
        done = summed / total
        for h in range(MEMBERS):
            store(t, h, done[:, h * TILE : (h + 1) * TILE].T.astype(jnp.bfloat16))

    def attend_by_maximum(t):
        row_max[...] = jnp.full(row_max.shape, NEG_FILL, jnp.float32)
        row_sum[...] = jnp.zeros(row_sum.shape, jnp.float32)
        acc[...] = jnp.zeros(acc.shape, jnp.float32)
        row = lax.broadcasted_iota(jnp.int32, (TILE, TILE), 0)
        column = lax.broadcasted_iota(jnp.int32, (TILE, TILE), 1)

        @pl.loop(0, counts[t])
        def _(i):
            tile = lists[t, i]
            k, v = keys[tile], values[tile]
            visible = (column <= row) | (i > 0)
            for h in range(MEMBERS):
                rows = slice(h * TILE, (h + 1) * TILE)
                scaled = scores(queries[t, rows, :], k) * SCALE
                before = row_max[rows, :]
                block_max = jnp.max(jnp.where(visible, scaled, NEG_FILL), axis=1, keepdims=True)
                after = jnp.maximum(before, block_max)
                weights = jnp.where(visible, jnp.exp(scaled - after), 0.0)
                factor = jnp.exp(before - after)
                row_sum[rows, :] = row_sum[rows, :] * factor + jnp.sum(weights, axis=1, keepdims=True)
                update = jnp.dot(weights.astype(jnp.bfloat16), v, preferred_element_type=jnp.float32)
                acc[rows, :] = acc[rows, :] * factor + update
                row_max[rows, :] = after

        for h in range(MEMBERS):
            rows = slice(h * TILE, (h + 1) * TILE)
            store(t, h, (acc[rows, :] / row_sum[rows, :]).astype(jnp.bfloat16))

    @pl.when(live < 2)
    def _():
        response_out[TILE:, :] = jnp.zeros((TILE, ROWS), jnp.bfloat16)

    sums[...] = jnp.ones(sums.shape, jnp.float32)
    row_tiles = jnp.where(live == 2, 3, 2)

    @pl.loop(0, row_tiles)
    def _(t):
        count = counts[t]
        for sure, size in zip((1,) + SIZES, SIZES):

            @pl.when((count <= size) if sure == 1 else (count > sure) & (count <= size))
            def _(sure=sure, size=size):
                attend(t, size, sure)

    fits = (jnp.min(sums[0:1, :]) > 1e-25) & (jnp.max(sums[1:2, :]) < 1e30)

    @pl.when(jnp.logical_not(fits))
    def _():
        @pl.loop(0, row_tiles)
        def _(t):
            attend_by_maximum(t)


def attend_local(place, prefix_mask, self_mask, prefix_q, response_q, own_kv, pieces):
    smem = pl.BlockSpec(memory_space=pltpu.SMEM)
    wide = MEMBERS * HEAD_WIDTH
    rows_p, rows_r = prefix_q.shape[0], response_q.shape[0]
    return pl.pallas_call(
        attend_kernel,
        grid=(GROUPS,),
        in_specs=[
            smem,
            smem,
            smem,
            pl.BlockSpec((rows_p, wide), lambda g: (0, g)),
            pl.BlockSpec((rows_r, wide), lambda g: (0, g)),
            pl.BlockSpec((2, rows_r, HEAD_WIDTH), lambda g: (0, 0, g)),
        ]
        + [pl.BlockSpec((4, 2, PART, HEAD_WIDTH), lambda g: (0, 0, 0, g))] * 8,
        out_specs=[
            pl.BlockSpec((rows_p, wide), lambda g: (0, g)),
            pl.BlockSpec((rows_r, wide), lambda g: (0, g)),
        ],
        out_shape=[
            jax.ShapeDtypeStruct(prefix_q.shape, jnp.bfloat16),
            jax.ShapeDtypeStruct(response_q.shape, jnp.bfloat16),
        ],
        scratch_shapes=[
            pltpu.VMEM((KEY_TILES, TILE, HEAD_WIDTH), jnp.bfloat16),
            pltpu.VMEM((KEY_TILES, TILE, HEAD_WIDTH), jnp.bfloat16),
            pltpu.VMEM((KEY_TILES, HEAD_WIDTH, TILE), jnp.bfloat16),
            pltpu.VMEM((3, ROWS, HEAD_WIDTH), jnp.bfloat16),
            pltpu.VMEM((8, ROWS), jnp.float32),
            pltpu.VMEM((ROWS, HEAD_WIDTH), jnp.float32),
            pltpu.VMEM((ROWS, HEAD_WIDTH), jnp.float32),
            pltpu.VMEM((ROWS, HEAD_WIDTH), jnp.float32),
            pltpu.SMEM((3, KEY_TILES + 2), jnp.int32),
            pltpu.SMEM((3,), jnp.int32),
        ],
        compiler_params=pltpu.CompilerParams(vmem_limit_bytes=40 * 1024 * 1024),
        cost_estimate=pl.CostEstimate(
            flops=8 * 10**9, bytes_accessed=8 * 10**6, transcendentals=15 * 10**6
        ),
    )(place, prefix_mask, self_mask, prefix_q, response_q, own_kv, *pieces)


def shards(
    prefix_query,
    prefix_cache,
    response_query,
    response_key_value_cache,
    response_tiles,
    prefix_mask,
    self_mask,
):
    rank = lax.axis_index("resp")
    half = lax.axis_index("tp")
    core = rank % 2
    x = (rank // 2) % 4
    y = half * 2 + rank // 8
    place = jnp.stack([x, y, core, rank, response_tiles[0]]).astype(jnp.int32)
    same_core, other_core = gather_prompt(prefix_cache, half, core)
    prefix_out, response_out = attend_local(
        place,
        prefix_mask[0],
        self_mask[0],
        prefix_query,
        response_query[0],
        response_key_value_cache[:, 0],
        same_core + other_core,
    )
    return prefix_out, response_out[None]


def solution(mesh):
    placed = (
        P(("prompt", "resp"), "tp"),
        P(None, ("prompt", "resp", "tp"), None),
        P(("prompt", "resp"), None, "tp"),
        P(None, ("prompt", "resp"), None, "tp"),
        P(("prompt", "resp")),
        P(("prompt", "resp"), None, None),
        P(("prompt", "resp"), None, None),
    )
    return jax.shard_map(
        shards,
        mesh=mesh,
        in_specs=placed,
        out_specs=(P(("prompt", "resp"), "tp"), P(("prompt", "resp"), None, "tp")),
        check_vma=False,
    )
```

time: 328 us -> 312 us (0.951)
  the two profiles are of different devices: /device:TPU:1 before, /device:TPU:141 now
where the time goes in v1:
time: 312 us
  Pallas kernels  267 us (86%)
  starting transfers between devices  35.2 us (11%)
  waiting for transfers between devices  6.2 us (2%)
    pallas_call x1, Pallas kernels, attend_local(): pl.pallas_call(attend_kernel, grid=(GROUPS,), in_specs=[smem, smem, smem,...  267 us
    ppermute x4, starting transfers between devices, gather_prompt(): other_core = [lax.ppermute(a, AX, CORE_PAIRS) for a in same_core]  17 us
    ppermute x3, starting transfers between devices, gather_prompt(): lax.ppermute(mine if m == 1 else other, AX, second_pairs(m))  9.25 us
    ppermute x3, starting transfers between devices, gather_prompt(): got = [cache] + [lax.ppermute(cache, AX, first_pairs(m)) for m in (1, 2, 3)]  8.98 us
  transfers between devices with their start and end apart: 10, of which 4 were waited for; matrix products, arithmetic and copies ran while one was open for 0% of the time, Pallas kernels for 0%

profile of v1, /device:TPU:141, one launch (start us, length us, event | category | flops | bytes accessed | tf_op | source)
XLA Modules:
  0.0 311.6 jit_solution(11893950204366097932)
XLA Ops:
  0.6 2.8 collective-permute-start
  3.5 1.9 collective-permute-start.2
  5.4 4.2 %collective-permute-start.1 = (bf16[2,64,1024]{2,1,0:T(8,128)(2,1)}, bf16[2,64,1024]{2,1,0:T(8,128)(2,1)S(1)}, u32[]{:S(2)}, u32[]{:S(2)}) collective-permute-start(bf16[2,64,1024]{2,1,0:T(8,128)(2,1)} %param.8), channel_id=1, source_target_pairs={{0,1},{2,10},{16,17},{18,26},{1,0},{3,11},{17,16},{19,27},{4,5},{6... | collective-permute-start | bytes 786440 | tf_op jit(solution)/shard_map/ppermute | solution.py:56
  9.7 0.0 collective-permute-done
  9.7 1.4 collective-permute-done.2
  11.1 3.1 %collective-permute-done.1 = bf16[2,64,1024]{2,1,0:T(8,128)(2,1)S(1)} collective-permute-done((bf16[2,64,1024]{2,1,0:T(8,128)(2,1)}, bf16[2,64,1024]{2,1,0:T(8,128)(2,1)S(1)}, u32[]{:S(2)}, u32[]{:S(2)}) %collective-permute-start.1) | collective-permute-done | bytes 262176 | tf_op jit(solution)/shard_map/ppermute | solution.py:56
  14.2 0.0 copy-start.2
  14.2 1.1 pad_maximum_fusion
  15.4 0.0 copy-start
  15.4 0.0 copy-start.1
  15.4 0.0 copy-start.3
  15.4 0.0 copy-start.4
  15.4 0.1 constant_dynamic-slice_fusion
  15.5 3.6 %collective-permute-start.5 = (bf16[4,2,64,512]{3,2,1,0:T(8,128)(2,1)S(1)}, bf16[4,2,64,512]{3,2,1,0:T(8,128)(2,1)S(1)}, u32[]{:S(2)}, u32[]{:S(2)}) collective-permute-start(bf16[4,2,64,512]{3,2,1,0:T(8,128)(2,1)S(1)} %get-tuple-element.6), channel_id=1, source_target_pairs={{0,12},{2,19},{16,28},{18,3},{1,13},{3,18},{17,29},{19,2},{4,8},{6... | collective-permute-start | bytes 1572872 | tf_op jit(solution)/shard_map/ppermute | solution.py:62
  19.2 2.6 collective-permute-start.4
  21.8 3.0 collective-permute-start.3
  24.8 6.4 %collective-permute-start.6 = (bf16[4,2,64,512]{3,2,1,0:T(8,128)(2,1)S(1)}, bf16[4,2,64,512]{3,2,1,0:T(8,128)(2,1)}, u32[]{:S(2)}, u32[]{:S(2)}) collective-permute-start(bf16[4,2,64,512]{3,2,1,0:T(8,128)(2,1)S(1)} %get-tuple-element.7.rest_0_), channel_id=1, source_target_pairs={{0,2},{2,0},{16,18},{18,16},{1,3},{3,1},{17,19},{19,17},{4,6},{6,4... | collective-permute-start | bytes 1572872 | tf_op jit(solution)/shard_map/ppermute | solution.py:64
  31.2 0.6 collective-permute-done.5.rest_3_
  31.7 6.3 %collective-permute-start.9 = (bf16[4,2,64,512]{3,2,1,0:T(8,128)(2,1)S(1)}, bf16[4,2,64,512]{3,2,1,0:T(8,128)(2,1)}, u32[]{:S(2)}, u32[]{:S(2)}) collective-permute-start(bf16[4,2,64,512]{3,2,1,0:T(8,128)(2,1)S(1)} %collective-permute-done.5.rest_3_), channel_id=1, source_target_pairs={{0,2},{2,0},{16,18},{18,16},{1,3},{3,1},{17,19},{19,17},{4,6},{6,4... | collective-permute-start | bytes 1572872 | tf_op jit(solution)/shard_map/ppermute | solution.py:64
  38.0 0.0 collective-permute-done.4.rest_2_
  38.0 1.9 collective-permute-start.8
  40.0 0.0 collective-permute-done.3.rest_1_
  40.0 2.4 collective-permute-start.7
  43.1 0.1 stack.34.place
  43.2 0.0 collective-permute-done.6.rest_4_
  43.2 0.0 collective-permute-done.9.rest_7_
  43.2 0.0 collective-permute-done.8.rest_6_
  43.2 1.1 collective-permute-done.7.rest_5_
  44.3 0.0 copy-done.2
  44.3 0.0 copy-done
  44.3 0.0 copy-done.1
  44.3 0.0 copy-done.3
  44.3 0.0 copy-done.4
  44.3 267.3 %shard_map.86 = (bf16[128,2560]{1,0:T(8,128)(2,1)}, bf16[256,2560]{1,0:T(8,128)(2,1)}) custom-call(s32[5]{0:T(128)S(1)} %stack.34.place, s32[2,16]{1,0:T(2,128)S(1)} %bitcast.15, s32[2,2]{1,0:T(2,128)S(1)} %bitcast.16, bf16[128,2560]{1,0:T(8,128)(2,1)S(1)} %copy-done.1, bf16[256,2560]{1,0:T(8,128)(2,1)S(1)} %bitcast.13, bf16[2,256,512]{2,1,0:T(8,128)(2,1)S(1)} %bitcast.14, ...), custom_call_target="tpu_custom_call" | custom-call | flops 8000000000 | bytes 8000000 | tf_op jit(solution)/shard_map/pallas_call | solution.py:227
Async XLA Ops:
  0.6 9.0 %collective-permute-start = (bf16[2,64,1024]{2,1,0:T(8,128)(2,1)}, bf16[2,64,1024]{2,1,0:T(8,128)(2,1)S(1)}, u32[]{:S(2)}, u32[]{:S(2)}) collective-permute-start(bf16[2,64,1024]{2,1,0:T(8,128)(2,1)} %param.8), channel_id=1, source_target_pairs={{0,16},{2,6},{16,0},{18,22},{1,17},{3,7},{17,1},{19,23},{4,20},{6,... | collective-permute-start | bytes 786440 | tf_op jit(solution)/shard_map/ppermute | solution.py:56
  3.5 7.6 %collective-permute-start.2 = (bf16[2,64,1024]{2,1,0:T(8,128)(2,1)}, bf16[2,64,1024]{2,1,0:T(8,128)(2,1)S(1)}, u32[]{:S(2)}, u32[]{:S(2)}) collective-permute-start(bf16[2,64,1024]{2,1,0:T(8,128)(2,1)} %param.8), channel_id=1, source_target_pairs={{0,17},{2,14},{16,1},{18,30},{1,16},{3,15},{17,0},{19,31},{4,21},{... | collective-permute-start | bytes 786440 | tf_op jit(solution)/shard_map/ppermute | solution.py:56
  5.4 8.8 %collective-permute-start.1 = (bf16[2,64,1024]{2,1,0:T(8,128)(2,1)}, bf16[2,64,1024]{2,1,0:T(8,128)(2,1)S(1)}, u32[]{:S(2)}, u32[]{:S(2)}) collective-permute-start(bf16[2,64,1024]{2,1,0:T(8,128)(2,1)} %param.8), channel_id=1, source_target_pairs={{0,1},{2,10},{16,17},{18,26},{1,0},{3,11},{17,16},{19,27},{4,5},{6... | collective-permute-start | bytes 786440 | tf_op jit(solution)/shard_map/ppermute | solution.py:56
  14.2 30.0 %copy-start.2 = (bf16[2,1,256,512]{3,2,1,0:T(8,128)(2,1)S(1)}, bf16[2,1,256,512]{3,2,1,0:T(8,128)(2,1)}, u32[]{:S(2)}) copy-start(bf16[2,1,256,512]{3,2,1,0:T(8,128)(2,1)} %param.10) | copy-start | bytes 1572868
  15.4 28.9 %copy-start = (bf16[1,256,2560]{2,1,0:T(8,128)(2,1)S(1)}, bf16[1,256,2560]{2,1,0:T(8,128)(2,1)}, u32[]{:S(2)}) copy-start(bf16[1,256,2560]{2,1,0:T(8,128)(2,1)} %param.9) | copy-start | bytes 3932164
  15.4 28.9 %copy-start.1 = (bf16[128,2560]{1,0:T(8,128)(2,1)S(1)}, bf16[128,2560]{1,0:T(8,128)(2,1)}, u32[]{:S(2)}) copy-start(bf16[128,2560]{1,0:T(8,128)(2,1)} %prefix_q.1) | copy-start | bytes 1966084
  15.4 28.9 %copy-start.3 = (s32[1,2,16]{2,1,0:T(2,128)S(1)}, s32[1,2,16]{2,1,0:T(2,128)}, u32[]{:S(2)}) copy-start(s32[1,2,16]{2,1,0:T(2,128)} %param.12) | copy-start | bytes 388
  15.4 28.9 %copy-start.4 = (s32[1,2,2]{2,1,0:T(2,128)S(1)}, s32[1,2,2]{2,1,0:T(2,128)}, u32[]{:S(2)}) copy-start(s32[1,2,2]{2,1,0:T(2,128)} %param.13) | copy-start | bytes 52
  15.5 16.2 %collective-permute-start.5 = (bf16[4,2,64,512]{3,2,1,0:T(8,128)(2,1)S(1)}, bf16[4,2,64,512]{3,2,1,0:T(8,128)(2,1)S(1)}, u32[]{:S(2)}, u32[]{:S(2)}) collective-permute-start(bf16[4,2,64,512]{3,2,1,0:T(8,128)(2,1)S(1)} %get-tuple-element.6), channel_id=1, source_target_pairs={{0,12},{2,19},{16,28},{18,3},{1,13},{3,18},{17,29},{19,2},{4,8},{6... | collective-permute-start | bytes 1572872 | tf_op jit(solution)/shard_map/ppermute | solution.py:62
  19.2 18.9 %collective-permute-start.4 = (bf16[4,2,64,512]{3,2,1,0:T(8,128)(2,1)S(1)}, bf16[4,2,64,512]{3,2,1,0:T(8,128)(2,1)}, u32[]{:S(2)}, u32[]{:S(2)}) collective-permute-start(bf16[4,2,64,512]{3,2,1,0:T(8,128)(2,1)S(1)} %get-tuple-element.6), channel_id=1, source_target_pairs={{0,8},{2,3},{16,24},{18,19},{1,9},{3,2},{17,25},{19,18},{4,12},{6,... | collective-permute-start | bytes 1572872 | tf_op jit(solution)/shard_map/ppermute | solution.py:62
  21.8 18.1 %collective-permute-start.3 = (bf16[4,2,64,512]{3,2,1,0:T(8,128)(2,1)S(1)}, bf16[4,2,64,512]{3,2,1,0:T(8,128)(2,1)}, u32[]{:S(2)}, u32[]{:S(2)}) collective-permute-start(bf16[4,2,64,512]{3,2,1,0:T(8,128)(2,1)S(1)} %get-tuple-element.7.rest_0_), channel_id=1, source_target_pairs={{0,4},{2,18},{16,20},{18,2},{1,5},{3,19},{17,21},{19,3},{4,0},{6,2... | collective-permute-start | bytes 1572872 | tf_op jit(solution)/shard_map/ppermute | solution.py:62
  24.8 18.4 %collective-permute-start.6 = (bf16[4,2,64,512]{3,2,1,0:T(8,128)(2,1)S(1)}, bf16[4,2,64,512]{3,2,1,0:T(8,128)(2,1)}, u32[]{:S(2)}, u32[]{:S(2)}) collective-permute-start(bf16[4,2,64,512]{3,2,1,0:T(8,128)(2,1)S(1)} %get-tuple-element.7.rest_0_), channel_id=1, source_target_pairs={{0,2},{2,0},{16,18},{18,16},{1,3},{3,1},{17,19},{19,17},{4,6},{6,4... | collective-permute-start | bytes 1572872 | tf_op jit(solution)/shard_map/ppermute | solution.py:64
  31.7 11.4 %collective-permute-start.9 = (bf16[4,2,64,512]{3,2,1,0:T(8,128)(2,1)S(1)}, bf16[4,2,64,512]{3,2,1,0:T(8,128)(2,1)}, u32[]{:S(2)}, u32[]{:S(2)}) collective-permute-start(bf16[4,2,64,512]{3,2,1,0:T(8,128)(2,1)S(1)} %collective-permute-done.5.rest_3_), channel_id=1, source_target_pairs={{0,2},{2,0},{16,18},{18,16},{1,3},{3,1},{17,19},{19,17},{4,6},{6,4... | collective-permute-start | bytes 1572872 | tf_op jit(solution)/shard_map/ppermute | solution.py:64
  38.0 5.1 %collective-permute-start.8 = (bf16[4,2,64,512]{3,2,1,0:T(8,128)(2,1)}, bf16[4,2,64,512]{3,2,1,0:T(8,128)(2,1)}, u32[]{:S(2)}, u32[]{:S(2)}) collective-permute-start(bf16[4,2,64,512]{3,2,1,0:T(8,128)(2,1)} %collective-permute-done.4.rest_2_), channel_id=1, source_target_pairs={{0,2},{2,0},{16,18},{18,16},{1,3},{3,1},{17,19},{19,17},{4,6},{6,4... | collective-permute-start | bytes 1572872 | tf_op jit(solution)/shard_map/ppermute | solution.py:64
  40.0 4.3 %collective-permute-start.7 = (bf16[4,2,64,512]{3,2,1,0:T(8,128)(2,1)}, bf16[4,2,64,512]{3,2,1,0:T(8,128)(2,1)}, u32[]{:S(2)}, u32[]{:S(2)}) collective-permute-start(bf16[4,2,64,512]{3,2,1,0:T(8,128)(2,1)} %collective-permute-done.3.rest_1_), channel_id=1, source_target_pairs={{0,2},{2,0},{16,18},{18,16},{1,3},{3,1},{17,19},{19,17},{4,6},{6,4... | collective-permute-start | bytes 1572872 | tf_op jit(solution)/shard_map/ppermute | solution.py:64

commit v2 on v1

--- a/solution.py
+++ b/solution.py
@@ -131,6 +131,15 @@
         def _():
             start = pl.multiple_of((t - 1) * TILE, TILE)
             response_out[pl.ds(start, TILE), columns] = block
+
+    def store_all(t, block):
+        @pl.when(t == 0)
+        def _():
+            prefix_out[...] = block
+
+        @pl.when(t > 0)
+        def _():
+            response_out[pl.ds(pl.multiple_of((t - 1) * TILE, TILE), TILE), :] = block
 
     def scores(a, b):
         return lax.dot_general(a, b, (((1,), (1,)), ((), ())), preferred_element_type=jnp.float32)
@@ -163,8 +172,8 @@
         sums[0:1, :] = jnp.minimum(sums[0:1, :], total)
         sums[1:2, :] = jnp.maximum(sums[1:2, :], total)
         done = summed / total
-        for h in range(MEMBERS):
-            store(t, h, done[:, h * TILE : (h + 1) * TILE].T.astype(jnp.bfloat16))
+        blocks = [done[:, h * TILE : (h + 1) * TILE].T.astype(jnp.bfloat16) for h in range(MEMBERS)]
+        store_all(t, jnp.concatenate(blocks, axis=1))
 
     def attend_by_maximum(t):
         row_max[...] = jnp.full(row_max.shape, NEG_FILL, jnp.float32)

time: 312 us -> 315 us (level)
  the two profiles are of different devices: /device:TPU:141 before, /device:TPU:302 now
where the time goes in v2:
time: 315 us; the launch traced here: 314 us
  Pallas kernels  269 us (85%)
  starting transfers between devices  27.9 us (9%)
  waiting for transfers between devices  14.4 us (5%)
    pallas_call x1, Pallas kernels, attend_local(): pl.pallas_call(attend_kernel, grid=(GROUPS,), in_specs=[smem, smem, smem,...  269 us
    ppermute x3, starting transfers between devices, gather_prompt(): lax.ppermute(mine if m == 1 else other, AX, second_pairs(m))  9.95 us
    ppermute x3, starting transfers between devices, gather_prompt(): got = [cache] + [lax.ppermute(cache, AX, first_pairs(m)) for m in (1, 2, 3)]  9.82 us
    ppermute x4, starting transfers between devices, gather_prompt(): other_core = [lax.ppermute(a, AX, CORE_PAIRS) for a in same_core]  8.16 us
    ppermute x3, waiting for transfers between devices, gather_prompt(): got = [cache] + [lax.ppermute(cache, AX, first_pairs(m)) for m in (1, 2, 3)]  6.8 us
  transfers between devices with their start and end apart: 10, of which 4 were waited for; matrix products, arithmetic and copies ran while one was open for 0% of the time, Pallas kernels for 0%

profile of v2, /device:TPU:302, one launch (start us, length us, event | category | flops | bytes accessed | tf_op | source)
XLA Modules:
  0.0 314.2 jit_solution(8269393356494523171)
XLA Ops:
  0.6 2.4 collective-permute-start
  3.0 4.3 %collective-permute-start.2 = (bf16[2,64,1024]{2,1,0:T(8,128)(2,1)}, bf16[2,64,1024]{2,1,0:T(8,128)(2,1)S(1)}, u32[]{:S(2)}, u32[]{:S(2)}) collective-permute-start(bf16[2,64,1024]{2,1,0:T(8,128)(2,1)} %param.8), channel_id=1, source_target_pairs={{0,17},{2,14},{16,1},{18,30},{1,16},{3,15},{17,0},{19,31},{4,21},{... | collective-permute-start | bytes 786440 | tf_op jit(solution)/shard_map/ppermute | solution.py:56
  7.3 3.1 %collective-permute-start.1 = (bf16[2,64,1024]{2,1,0:T(8,128)(2,1)}, bf16[2,64,1024]{2,1,0:T(8,128)(2,1)S(1)}, u32[]{:S(2)}, u32[]{:S(2)}) collective-permute-start(bf16[2,64,1024]{2,1,0:T(8,128)(2,1)} %param.8), channel_id=1, source_target_pairs={{0,1},{2,10},{16,17},{18,26},{1,0},{3,11},{17,16},{19,27},{4,5},{6... | collective-permute-start | bytes 786440 | tf_op jit(solution)/shard_map/ppermute | solution.py:56
  10.5 0.0 collective-permute-done
  10.5 1.4 collective-permute-done.2
  11.9 5.4 %collective-permute-done.1 = bf16[2,64,1024]{2,1,0:T(8,128)(2,1)S(1)} collective-permute-done((bf16[2,64,1024]{2,1,0:T(8,128)(2,1)}, bf16[2,64,1024]{2,1,0:T(8,128)(2,1)S(1)}, u32[]{:S(2)}, u32[]{:S(2)}) %collective-permute-start.1) | collective-permute-done | bytes 262176 | tf_op jit(solution)/shard_map/ppermute | solution.py:56
  17.3 0.0 copy-start.2
  17.3 1.1 pad_maximum_fusion
  18.4 0.0 copy-start
  18.5 0.0 copy-start.1
  18.5 0.0 copy-start.3
  18.5 0.0 copy-start.4
  18.5 0.1 constant_dynamic-slice_fusion
  18.6 2.5 collective-permute-start.5
  21.1 4.3 %collective-permute-start.4 = (bf16[4,2,64,512]{3,2,1,0:T(8,128)(2,1)S(1)}, bf16[4,2,64,512]{3,2,1,0:T(8,128)(2,1)}, u32[]{:S(2)}, u32[]{:S(2)}) collective-permute-start(bf16[4,2,64,512]{3,2,1,0:T(8,128)(2,1)S(1)} %get-tuple-element.6), channel_id=1, source_target_pairs={{0,8},{2,3},{16,24},{18,19},{1,9},{3,2},{17,25},{19,18},{4,12},{6,... | collective-permute-start | bytes 1572872 | tf_op jit(solution)/shard_map/ppermute | solution.py:62
  25.5 3.1 collective-permute-start.3
  28.6 1.9 collective-permute-start.6
  30.5 6.1 %collective-permute-done.5.rest_3_ = bf16[4,2,64,512]{3,2,1,0:T(8,128)(2,1)S(1)} collective-permute-done((bf16[4,2,64,512]{3,2,1,0:T(8,128)(2,1)S(1)}, bf16[4,2,64,512]{3,2,1,0:T(8,128)(2,1)S(1)}, u32[]{:S(2)}, u32[]{:S(2)}) %collective-permute-start.5) | collective-permute-done | bytes 524320 | tf_op jit(solution)/shard_map/ppermute | solution.py:62
  36.7 1.9 collective-permute-start.9
  38.6 0.0 collective-permute-done.4.rest_2_
  38.6 2.4 collective-permute-start.8
  41.0 0.0 collective-permute-done.3.rest_1_
  41.0 1.9 collective-permute-start.7
  43.6 0.1 stack.34.place
  43.7 0.0 collective-permute-done.6.rest_4_
  43.7 0.0 collective-permute-done.9.rest_7_
  43.7 0.0 collective-permute-done.8.rest_6_
  43.7 1.4 collective-permute-done.7.rest_5_
  45.2 0.0 copy-done.2
  45.2 0.0 copy-done
  45.2 0.0 copy-done.1
  45.2 0.0 copy-done.3
  45.2 0.0 copy-done.4
  45.2 269.0 %shard_map.86 = (bf16[128,2560]{1,0:T(8,128)(2,1)}, bf16[256,2560]{1,0:T(8,128)(2,1)}) custom-call(s32[5]{0:T(128)S(1)} %stack.34.place, s32[2,16]{1,0:T(2,128)S(1)} %bitcast.15, s32[2,2]{1,0:T(2,128)S(1)} %bitcast.16, bf16[128,2560]{1,0:T(8,128)(2,1)S(1)} %copy-done.1, bf16[256,2560]{1,0:T(8,128)(2,1)S(1)} %bitcast.13, bf16[2,256,512]{2,1,0:T(8,128)(2,1)S(1)} %bitcast.14, ...), custom_call_target="tpu_custom_call" | custom-call | flops 8000000000 | bytes 8000000 | tf_op jit(solution)/shard_map/pallas_call | solution.py:236
Async XLA Ops:
  0.6 9.9 %collective-permute-start = (bf16[2,64,1024]{2,1,0:T(8,128)(2,1)}, bf16[2,64,1024]{2,1,0:T(8,128)(2,1)S(1)}, u32[]{:S(2)}, u32[]{:S(2)}) collective-permute-start(bf16[2,64,1024]{2,1,0:T(8,128)(2,1)} %param.8), channel_id=1, source_target_pairs={{0,16},{2,6},{16,0},{18,22},{1,17},{3,7},{17,1},{19,23},{4,20},{6,... | collective-permute-start | bytes 786440 | tf_op jit(solution)/shard_map/ppermute | solution.py:56
  3.0 8.9 %collective-permute-start.2 = (bf16[2,64,1024]{2,1,0:T(8,128)(2,1)}, bf16[2,64,1024]{2,1,0:T(8,128)(2,1)S(1)}, u32[]{:S(2)}, u32[]{:S(2)}) collective-permute-start(bf16[2,64,1024]{2,1,0:T(8,128)(2,1)} %param.8), channel_id=1, source_target_pairs={{0,17},{2,14},{16,1},{18,30},{1,16},{3,15},{17,0},{19,31},{4,21},{... | collective-permute-start | bytes 786440 | tf_op jit(solution)/shard_map/ppermute | solution.py:56
  7.3 10.0 %collective-permute-start.1 = (bf16[2,64,1024]{2,1,0:T(8,128)(2,1)}, bf16[2,64,1024]{2,1,0:T(8,128)(2,1)S(1)}, u32[]{:S(2)}, u32[]{:S(2)}) collective-permute-start(bf16[2,64,1024]{2,1,0:T(8,128)(2,1)} %param.8), channel_id=1, source_target_pairs={{0,1},{2,10},{16,17},{18,26},{1,0},{3,11},{17,16},{19,27},{4,5},{6... | collective-permute-start | bytes 786440 | tf_op jit(solution)/shard_map/ppermute | solution.py:56
  17.3 27.9 %copy-start.2 = (bf16[2,1,256,512]{3,2,1,0:T(8,128)(2,1)S(1)}, bf16[2,1,256,512]{3,2,1,0:T(8,128)(2,1)}, u32[]{:S(2)}) copy-start(bf16[2,1,256,512]{3,2,1,0:T(8,128)(2,1)} %param.10) | copy-start | bytes 1572868
  18.4 26.7 %copy-start = (bf16[1,256,2560]{2,1,0:T(8,128)(2,1)S(1)}, bf16[1,256,2560]{2,1,0:T(8,128)(2,1)}, u32[]{:S(2)}) copy-start(bf16[1,256,2560]{2,1,0:T(8,128)(2,1)} %param.9) | copy-start | bytes 3932164
  18.5 26.7 %copy-start.1 = (bf16[128,2560]{1,0:T(8,128)(2,1)S(1)}, bf16[128,2560]{1,0:T(8,128)(2,1)}, u32[]{:S(2)}) copy-start(bf16[128,2560]{1,0:T(8,128)(2,1)} %prefix_q.1) | copy-start | bytes 1966084
  18.5 26.7 %copy-start.3 = (s32[1,2,16]{2,1,0:T(2,128)S(1)}, s32[1,2,16]{2,1,0:T(2,128)}, u32[]{:S(2)}) copy-start(s32[1,2,16]{2,1,0:T(2,128)} %param.12) | copy-start | bytes 388
  18.5 26.7 %copy-start.4 = (s32[1,2,2]{2,1,0:T(2,128)S(1)}, s32[1,2,2]{2,1,0:T(2,128)}, u32[]{:S(2)}) copy-start(s32[1,2,2]{2,1,0:T(2,128)} %param.13) | copy-start | bytes 52
  18.6 18.0 %collective-permute-start.5 = (bf16[4,2,64,512]{3,2,1,0:T(8,128)(2,1)S(1)}, bf16[4,2,64,512]{3,2,1,0:T(8,128)(2,1)S(1)}, u32[]{:S(2)}, u32[]{:S(2)}) collective-permute-start(bf16[4,2,64,512]{3,2,1,0:T(8,128)(2,1)S(1)} %get-tuple-element.6), channel_id=1, source_target_pairs={{0,12},{2,19},{16,28},{18,3},{1,13},{3,18},{17,29},{19,2},{4,8},{6... | collective-permute-start | bytes 1572872 | tf_op jit(solution)/shard_map/ppermute | solution.py:62
  21.1 17.4 %collective-permute-start.4 = (bf16[4,2,64,512]{3,2,1,0:T(8,128)(2,1)S(1)}, bf16[4,2,64,512]{3,2,1,0:T(8,128)(2,1)}, u32[]{:S(2)}, u32[]{:S(2)}) collective-permute-start(bf16[4,2,64,512]{3,2,1,0:T(8,128)(2,1)S(1)} %get-tuple-element.6), channel_id=1, source_target_pairs={{0,8},{2,3},{16,24},{18,19},{1,9},{3,2},{17,25},{19,18},{4,12},{6,... | collective-permute-start | bytes 1572872 | tf_op jit(solution)/shard_map/ppermute | solution.py:62
  25.5 15.5 %collective-permute-start.3 = (bf16[4,2,64,512]{3,2,1,0:T(8,128)(2,1)S(1)}, bf16[4,2,64,512]{3,2,1,0:T(8,128)(2,1)}, u32[]{:S(2)}, u32[]{:S(2)}) collective-permute-start(bf16[4,2,64,512]{3,2,1,0:T(8,128)(2,1)S(1)} %get-tuple-element.7.rest_0_), channel_id=1, source_target_pairs={{0,4},{2,18},{16,20},{18,2},{1,5},{3,19},{17,21},{19,3},{4,0},{6,2... | collective-permute-start | bytes 1572872 | tf_op jit(solution)/shard_map/ppermute | solution.py:62
  28.6 15.1 %collective-permute-start.6 = (bf16[4,2,64,512]{3,2,1,0:T(8,128)(2,1)S(1)}, bf16[4,2,64,512]{3,2,1,0:T(8,128)(2,1)}, u32[]{:S(2)}, u32[]{:S(2)}) collective-permute-start(bf16[4,2,64,512]{3,2,1,0:T(8,128)(2,1)S(1)} %get-tuple-element.7.rest_0_), channel_id=1, source_target_pairs={{0,2},{2,0},{16,18},{18,16},{1,3},{3,1},{17,19},{19,17},{4,6},{6,4... | collective-permute-start | bytes 1572872 | tf_op jit(solution)/shard_map/ppermute | solution.py:64
  36.7 7.1 %collective-permute-start.9 = (bf16[4,2,64,512]{3,2,1,0:T(8,128)(2,1)S(1)}, bf16[4,2,64,512]{3,2,1,0:T(8,128)(2,1)}, u32[]{:S(2)}, u32[]{:S(2)}) collective-permute-start(bf16[4,2,64,512]{3,2,1,0:T(8,128)(2,1)S(1)} %collective-permute-done.5.rest_3_), channel_id=1, source_target_pairs={{0,2},{2,0},{16,18},{18,16},{1,3},{3,1},{17,19},{19,17},{4,6},{6,4... | collective-permute-start | bytes 1572872 | tf_op jit(solution)/shard_map/ppermute | solution.py:64
  38.6 5.1 %collective-permute-start.8 = (bf16[4,2,64,512]{3,2,1,0:T(8,128)(2,1)}, bf16[4,2,64,512]{3,2,1,0:T(8,128)(2,1)}, u32[]{:S(2)}, u32[]{:S(2)}) collective-permute-start(bf16[4,2,64,512]{3,2,1,0:T(8,128)(2,1)} %collective-permute-done.4.rest_2_), channel_id=1, source_target_pairs={{0,2},{2,0},{16,18},{18,16},{1,3},{3,1},{17,19},{19,17},{4,6},{6,4... | collective-permute-start | bytes 1572872 | tf_op jit(solution)/shard_map/ppermute | solution.py:64
  41.0 4.1 %collective-permute-start.7 = (bf16[4,2,64,512]{3,2,1,0:T(8,128)(2,1)}, bf16[4,2,64,512]{3,2,1,0:T(8,128)(2,1)}, u32[]{:S(2)}, u32[]{:S(2)}) collective-permute-start(bf16[4,2,64,512]{3,2,1,0:T(8,128)(2,1)} %collective-permute-done.3.rest_1_), channel_id=1, source_target_pairs={{0,2},{2,0},{16,18},{18,16},{1,3},{3,1},{17,19},{19,17},{4,6},{6,4... | collective-permute-start | bytes 1572872 | tf_op jit(solution)/shard_map/ppermute | solution.py:64
